TPU v7x, 32 devices: a whole 2x2x4 slice. The times are simulated.
32 devices in a mesh: hours: 4 (over y, core), surf: 8 (over z, x).
Axes of the slice: x: 2, y: 2, z: 4, core: 2. Of those that a mesh axis runs over, the one named last changes fastest.
Arguments:
- sky_radiance: bfloat16 [256, 2304], P('hours'), parts along dimension 0, may hold values from 0.049804688 to 20
- surf_coeff: bfloat16 [128, 8, 128, 128], P('surf'), may hold values from 0 to 0.001953125
- surf_patch: int32 [128, 8], P('surf'), may hold values from 0 to 17
- surf_count: int32 [128], P('surf'), may hold values from 1 to 8, as said below
- sens_coeff: bfloat16 [192, 8, 128, 128], P('surf'), may hold values from 0 to 0.001953125
- sens_patch: int32 [192, 8], P('surf'), may hold values from 0 to 17
- sens_count: int32 [192], P('surf'), may hold values from 1 to 8, as said below
- albedo: float32 [16384], P('surf'), may hold values from 0.08 to 0.8
- view_tile: bfloat16 [128, 8, 128, 128], P('surf')
- view_peer: int32 [128, 8], P('surf'), may hold values from 0 to 7, as said below
- wanted: int32 [8, 8], P('surf'), may hold values from 0 to 15
- sens_surf: int32 [2, 24576], P(None, 'surf'), may hold values from 0 to 16383, as said below
- sens_weight: float32 [2, 24576], P(None, 'surf'), may hold values from 0.2 to 1
Outputs:
- surf_irradiance: float32 [256, 16384], P('hours', 'surf'), parts along dimension 0
- sens_irradiance: float32 [256, 24576], P('hours', 'surf'), parts along dimension 0
There are 4 independent parts, one for each index of `hours`. A program takes and returns all parts, laid end to end along the dimension named above; an argument that names none is the same for every part. Nothing has to cross between parts.
Inputs may be any that keep to these rules, and one draw needn't show every extreme that they name: `surf_count`: at least 1 and at most 8; some block has 8. `sens_count`: at least 1 and at most 8; some block has 8. `view_peer`: the 128 entries of one device name every device at least once. `sens_surf`: each sensor's surfaces lie on the device that holds the sensor.
All inputs are finite; a program needn't handle non-finite values.
Results may differ from a plain program's by a relative error of at most 0.0003.
Values may be sent and summed in bfloat16 or wider, within the bound.
A program may use at most 128 MiB of HBM per device.

v0:
```python
import functools

import jax
import jax.numpy as jnp
from jax import lax
from jax.experimental import pallas as pl
from jax.experimental.pallas import tpu as pltpu
from jax.sharding import PartitionSpec as P

F32 = jnp.float32
BF16 = jnp.bfloat16


def wide_dot(table, picks, weights):
    lhs = jnp.concatenate([table[i] for i in picks], axis=1)
    return jnp.dot(lhs, weights, preferred_element_type=F32)


def kernel(
    n,
    sky_hbm,
    surf_hbm,
    surf_patch_hbm,
    surf_count_hbm,
    sens_hbm,
    sens_patch_hbm,
    sens_count_hbm,
    albedo_hbm,
    view_hbm,
    view_peer_hbm,
    wanted_row,
    sens_surf_hbm,
    sens_weight_hbm,
    surf_hbm_out,
    sens_hbm_out,
    surf_out,
    sens_out,
    onehot,
    sky,
    surf_patch,
    surf_count,
    sens_patch,
    sens_count,
    albedo,
    view_peer,
    sens_surf,
    sens_weight,
    sky_tab,
    surf_w,
    sens_w,
    view_w,
    direct,
    rad,
    refl,
    send_a,
    send_b,
    slots_a,
    slots_b,
    want_v,
    want_s,
    small_sem,
    load_sem,
    out_sem,
    want_sem,
    send_sem,
    recv_sem,
):
    hours, patch_width = sky.shape
    blocks, depth, tile = view_w.shape
    sens_blocks = sens_w.shape[0]
    per = depth // tile
    patches = patch_width // tile
    me = lax.axis_index("surf")

    def peer(step):
        return lax.rem(me + step, n)

    barrier = pltpu.get_barrier_semaphore()

    def greet(step, carry):
        pl.semaphore_signal(
            barrier, inc=1, device_id={"surf": peer(step)}, device_id_type=pl.DeviceIdType.MESH
        )
        return carry

    lax.fori_loop(1, n, greet, 0)

    surf_parts = load_parts(blocks)
    sens_parts = load_parts(sens_blocks)

    def part(hbm, vmem, parts, i, first):
        size = vmem.shape[0] // parts
        span = pl.ds(i * size, size)
        return pltpu.make_async_copy(hbm.at[span], vmem.at[span], load_sem.at[first + i])

    surf_loads = [part(surf_hbm, surf_w, surf_parts, i, 0) for i in range(surf_parts)]
    view_load = part(view_hbm, view_w, 1, 0, surf_parts)
    sens_loads = [
        part(sens_hbm, sens_w, sens_parts, i, surf_parts + 1) for i in range(sens_parts)
    ]
    small = (
        (sky_hbm, sky),
        (surf_patch_hbm, surf_patch),
        (surf_count_hbm, surf_count),
        (albedo_hbm, albedo),
        (view_peer_hbm, view_peer),
        (sens_patch_hbm, sens_patch),
        (sens_count_hbm, sens_count),
        (sens_surf_hbm, sens_surf),
        (sens_weight_hbm, sens_weight),
    )
    small_loads = [
        pltpu.make_async_copy(src, dst, small_sem.at[i]) for i, (src, dst) in enumerate(small)
    ]
    early, late = small_loads[:4], small_loads[4:]
    for copy in (*early, *surf_loads, *late, *sens_loads[:2], view_load, *sens_loads[2:]):
        copy.start()

    small_loads[0].wait()
    for j in range(patches):
        sky_tab[j] = sky[:, j * tile : (j + 1) * tile]
    sky_tab[patches] = jnp.zeros((hours, tile), BF16)

    def remote(src, dst, kind, to, mine):
        return pltpu.make_async_remote_copy(
            src_ref=src,
            dst_ref=dst.at[mine],
            send_sem=send_sem.at[kind, to],
            recv_sem=recv_sem.at[kind, mine],
            device_id={"surf": to},
            device_id_type=pl.DeviceIdType.MESH,
        )

    def loop(low, high, body, group):
        count = high - low
        group = next(g for g in range(min(group, count), 0, -1) if count % g == 0)

        def go(i, carry):
            for u in range(group):
                body(low + i * group + u)
            return carry

        lax.fori_loop(0, count // group, go, 0)

    def each_peer(body):
        loop(1, n, lambda step: body(peer(step)), 7)

    def live(patch, count, k, b):
        return jnp.where(k < count[b], patch[k, b], patches)

    def direct_block(b):
        picks = [live(surf_patch, surf_count, k, b) for k in range(per)]
        value = wide_dot(sky_tab, picks, surf_w[b])
        direct[b] = value
        rad[b] = (value * albedo[b]).astype(BF16)

    def sens_block(b):
        picks = [live(sens_patch, sens_count, k, b) for k in range(per)]
        cols = pl.ds(pl.multiple_of(b * tile, tile), tile)
        sens_out[:, cols] = wide_dot(sky_tab, picks, sens_w[b])

    for copy in early[1:]:
        copy.wait()
    for i, copy in enumerate(surf_loads):
        if i == surf_parts // 2:
            pl.semaphore_wait(barrier, n - 1)
            each_peer(lambda e: remote(wanted_row.at[0], want_v, 0, e, me).start())
            own_row = pltpu.make_async_copy(wanted_row.at[0], want_v.at[me], want_sem.at[0])
            own_row.start()
        copy.wait()
        size = blocks // surf_parts
        loop(i * size, (i + 1) * size, direct_block, 4)

    for copy in late:
        copy.wait()
    own_row.wait()
    each_peer(lambda e: remote(wanted_row.at[0], want_v, 0, me, e).wait_recv())
    to_smem = pltpu.make_async_copy(want_v, want_s, want_sem.at[1])
    to_smem.start()
    to_smem.wait()

    def asked(e):
        return want_s[e, 0, me]

    def first_send(e):
        send_a[e] = rad[asked(e)]
        remote(send_a.at[e], slots_a, 1, e, me).start()

    each_peer(first_send)
    slots_a[me] = rad[asked(me)]

    half = sens_parts // 2
    rows = lax.broadcasted_iota(jnp.int32, (tile, 2 * tile), 0)

    def onehot_block(r):
        cols = pl.ds(pl.multiple_of(r * tile, tile), tile)
        index = sens_surf[:, cols] - me * (blocks * tile)
        index = jnp.concatenate([index[0:1], index[1:2]], axis=1)
        for s in range(blocks):
            hit = rows == index - s * tile
            onehot[r, s * tile : (s + 1) * tile, :] = jnp.where(hit, 1.0, 0.0).astype(BF16)

    def sens_part(i):
        sens_loads[i].wait()
        size = sens_blocks // sens_parts
        loop(i * size, (i + 1) * size, sens_block, 6)
        loop(i * size, (i + 1) * size, onehot_block, 1)

    for i in range(half):
        sens_part(i)

    each_peer(lambda e: remote(send_a.at[e], slots_a, 1, me, e).wait_recv())
    view_load.wait()

    def bounced(slots, b):
        picks = [view_peer[k, b] for k in range(per)]
        return wide_dot(slots, picks, view_w[b])

    def second_value(b):
        value = direct[b] + bounced(slots_a, b)
        return (value * albedo[b]).astype(BF16)

    def second_send(e):
        send_b[e] = second_value(asked(e))
        remote(send_b.at[e], slots_b, 2, e, me).start()

    each_peer(second_send)
    slots_b[me] = second_value(asked(me))

    for i in range(half, sens_parts):
        sens_part(i)

    each_peer(lambda e: remote(send_b.at[e], slots_b, 2, me, e).wait_recv())

    def last_block(b):
        value = bounced(slots_b, b)
        cols = pl.ds(pl.multiple_of(b * tile, tile), tile)
        high = value.astype(BF16)
        refl[:hours, cols] = high
        refl[hours:, cols] = (value - high.astype(F32)).astype(BF16)
        surf_out[:, cols] = direct[b] + value

    loop(0, blocks, last_block, 8)

    surf_store = pltpu.make_async_copy(surf_out, surf_hbm_out, out_sem.at[0])
    surf_store.start()

    def near_block(r):
        cols = pl.ds(pl.multiple_of(r * tile, tile), tile)
        both = jnp.dot(refl[...], onehot[r], preferred_element_type=F32)
        found = both[:hours] + both[hours:]
        weight = sens_weight[:, cols]
        sens_out[:, cols] = (
            sens_out[:, cols]
            + weight[0:1] * found[:, :tile]
            + weight[1:2] * found[:, tile:]
        )

    stores = [surf_store]
    for i in range(sens_parts):
        size = sens_blocks // sens_parts
        loop(i * size, (i + 1) * size, near_block, 3)
        cols = pl.ds(i * size * tile, size * tile)
        copy = pltpu.make_async_copy(
            sens_out.at[:, cols], sens_hbm_out.at[:, cols], out_sem.at[1 + i]
        )
        copy.start()
        stores.append(copy)
    for copy in stores:
        copy.wait()

    each_peer(lambda e: remote(wanted_row.at[0], want_v, 0, e, me).wait_send())
    each_peer(lambda e: remote(send_a.at[e], slots_a, 1, e, me).wait_send())
    each_peer(lambda e: remote(send_b.at[e], slots_b, 2, e, me).wait_send())


def load_parts(blocks):
    return 4 if blocks % 4 == 0 else 1


def local(
    sky_radiance,
    surf_coeff,
    surf_patch,
    surf_count,
    sens_coeff,
    sens_patch,
    sens_count,
    albedo,
    view_tile,
    view_peer,
    wanted,
    sens_surf,
    sens_weight,
):
    n = lax.axis_size("surf")
    hours, patch_width = sky_radiance.shape
    blocks, per, tile, _ = view_tile.shape
    sens_blocks = sens_coeff.shape[0]
    depth = per * tile
    patches = patch_width // tile

    hbm = pl.BlockSpec(memory_space=pltpu.HBM)
    loads = load_parts(blocks) + 1 + load_parts(sens_blocks)
    made = pl.pallas_call(
        functools.partial(kernel, n),
        out_shape=(
            jax.ShapeDtypeStruct((hours, blocks * tile), F32),
            jax.ShapeDtypeStruct((hours, sens_blocks * tile), F32),
        ),
        in_specs=[hbm] * 13,
        out_specs=(hbm, hbm),
        scratch_shapes=[
            pltpu.VMEM((hours, blocks * tile), F32),
            pltpu.VMEM((hours, sens_blocks * tile), F32),
            pltpu.VMEM((sens_blocks, blocks * tile, 2 * tile), BF16),
            pltpu.VMEM((hours, patch_width), BF16),
            pltpu.SMEM((per, blocks), jnp.int32),
            pltpu.SMEM((blocks,), jnp.int32),
            pltpu.SMEM((per, sens_blocks), jnp.int32),
            pltpu.SMEM((sens_blocks,), jnp.int32),
            pltpu.VMEM((blocks, 1, tile), F32),
            pltpu.SMEM((per, blocks), jnp.int32),
            pltpu.VMEM(sens_surf.shape, jnp.int32),
            pltpu.VMEM(sens_weight.shape, F32),
            pltpu.VMEM((patches + 1, hours, tile), BF16),
            pltpu.VMEM((blocks, depth, tile), BF16),
            pltpu.VMEM((sens_blocks, depth, tile), BF16),
            pltpu.VMEM((blocks, depth, tile), BF16),
            pltpu.VMEM((blocks, hours, tile), F32),
            pltpu.VMEM((blocks, hours, tile), BF16),
            pltpu.VMEM((2 * hours, blocks * tile), BF16),
            pltpu.VMEM((n, hours, tile), BF16),
            pltpu.VMEM((n, hours, tile), BF16),
            pltpu.VMEM((n, hours, tile), BF16),
            pltpu.VMEM((n, hours, tile), BF16),
            pltpu.VMEM((n, 1, n), jnp.int32),
            pltpu.SMEM((n, 1, n), jnp.int32),
            pltpu.SemaphoreType.DMA((9,)),
            pltpu.SemaphoreType.DMA((loads,)),
            pltpu.SemaphoreType.DMA((1 + load_parts(sens_blocks),)),
            pltpu.SemaphoreType.DMA((2,)),
            pltpu.SemaphoreType.DMA((3, n)),
            pltpu.SemaphoreType.DMA((3, n)),
        ],
        compiler_params=pltpu.CompilerParams(
            collective_id=0, has_side_effects=True, vmem_limit_bytes=62 * 2**20
        ),
    )(
        sky_radiance,
        surf_coeff.reshape(blocks, depth, tile),
        surf_patch.T,
        surf_count,
        sens_coeff.reshape(sens_blocks, depth, tile),
        sens_patch.T,
        sens_count,
        albedo.reshape(blocks, 1, tile),
        view_tile.reshape(blocks, depth, tile),
        view_peer.T,
        wanted.reshape(1, 1, n),
        sens_surf,
        sens_weight,
    )
    return hand_out(*made)


def hand_out(*arrays):
    parts = 4

    def body(*refs):
        count = len(arrays)
        held = refs[2 * count : 3 * count]
        sems = refs[-1]
        gets, puts = [], []
        for a in range(count):
            rows = arrays[a].shape[0] // parts
            for i in range(parts):
                span = pl.ds(i * rows, rows)
                at = a * parts + i
                gets.append(
                    pltpu.make_async_copy(refs[a].at[span], held[a].at[span], sems.at[0, at])
                )
                puts.append(
                    pltpu.make_async_copy(
                        held[a].at[span], refs[count + a].at[span], sems.at[1, at]
                    )
                )
        for get in gets:
            get.start()
        for get, put in zip(gets, puts):
            get.wait()
            put.start()
        for put in puts:
            put.wait()

    hbm = pl.BlockSpec(memory_space=pltpu.HBM)
    return pl.pallas_call(
        body,
        out_shape=tuple(jax.ShapeDtypeStruct(a.shape, a.dtype) for a in arrays),
        in_specs=[hbm] * len(arrays),
        out_specs=(hbm,) * len(arrays),
        scratch_shapes=[
            *(pltpu.VMEM(a.shape, a.dtype) for a in arrays),
            pltpu.SemaphoreType.DMA((2, parts * len(arrays))),
        ],
    )(*arrays)


def solution(mesh):
    in_specs = (
        P("hours", None),
        P("surf", None, None, None),
        P("surf", None),
        P("surf"),
        P("surf", None, None, None),
        P("surf", None),
        P("surf"),
        P("surf"),
        P("surf", None, None, None),
        P("surf", None),
        P("surf", None),
        P(None, "surf"),
        P(None, "surf"),
    )
    out_specs = (P("hours", "surf"), P("hours", "surf"))
    return jax.shard_map(local, mesh=mesh, in_specs=in_specs, out_specs=out_specs, check_vma=False)
```

profile of v0, /device:TPU:0, one launch (start us, length us, event | category | flops | bytes accessed | tf_op | source)
XLA Modules:
  0.0 30.2 jit_solution(8236134584880684311)
XLA Ops:
  0.6 27.3 %shard_map.140 = (f32[64,2048]{1,0:T(8,128)}, f32[64,3072]{1,0:T(8,128)}) custom-call(bf16[64,2304]{1,0:T(8,128)(2,1)} %sky_hbm.1, bf16[16,1024,128]{2,1,0:T(8,128)(2,1)} %bitcast.9, s32[8,16]{1,0:T(8,128)} %bitcast.12, s32[16]{0:T(128)} %surf_count_hbm.1, bf16[24,1024,128]{2,1,0:T(8,128)(2,1)} %bitcast.8, s32[8,24]{1,0:T(8,128)} %bitcast.13, ...), custom_call_target="tpu_custom_call" | custom-call | tf_op jit(solution)/shard_map/pallas_call | solution.py:305
  28.0 2.2 %shard_map.141 = (f32[64,2048]{1,0:T(8,128)}, f32[64,3072]{1,0:T(8,128)}) custom-call(f32[64,2048]{1,0:T(8,128)} %get-tuple-element.4.refs_0_, f32[64,3072]{1,0:T(8,128)} %get-tuple-element.5.refs_1_), custom_call_target="tpu_custom_call" | custom-call | tf_op jit(solution)/shard_map/pallas_call | solution.py:397
where the time goes:
time: 30.3 us; the launch traced here: 30.2 us
  Pallas kernels  29.5 us (97%)
  between operations  0.64 us (2%)
    pallas_call x1, Pallas kernels, local(): pl.pallas_call(functools.partial(kernel, n), out_shape=(jax.ShapeDtypeStr...  27.3 us
    pallas_call x1, Pallas kernels, hand_out(): pl.pallas_call(body, out_shape=tuple((jax.ShapeDtypeStruct(a.shape, a.dty...  2.2 us

commit v1 on v0

v1 whole, which is shorter than its diff:
```python
import functools

import jax
import jax.numpy as jnp
from jax import lax
from jax.experimental import pallas as pl
from jax.experimental.pallas import tpu as pltpu
from jax.sharding import PartitionSpec as P

F32 = jnp.float32
BF16 = jnp.bfloat16
F8 = jnp.float8_e4m3fn

TOP = 256.0
STEP = 32.0


def wide_dot(table, picks, weights):
    lhs = jnp.concatenate([table[i] for i in picks], axis=1)
    return jnp.dot(lhs, weights, preferred_element_type=F32)


def farthest_first(n):
    if n > 8 or n & (n - 1):
        return None
    return [*range(n - 1, 0, -2), *range(n - 2, 0, -2)]


def kernel(
    n,
    sky_hbm,
    surf_hbm,
    surf_patch_hbm,
    surf_count_hbm,
    sens_hbm,
    sens_patch_hbm,
    sens_count_hbm,
    albedo_hbm,
    view_hbm,
    view_peer_hbm,
    wanted_hbm,
    sens_surf_hbm,
    sens_weight_hbm,
    surf_out,
    sens_out,
    pieces,
    onehot,
    gain,
    sky,
    surf_patch,
    surf_count,
    sens_patch,
    sens_count,
    albedo,
    view_peer,
    sens_surf,
    sens_weight,
    sky_tab,
    surf_w,
    sens_w,
    view_w,
    direct,
    rad,
    refl,
    send_a,
    send_b,
    slots_a,
    slots_b,
    want_own,
    want_v,
    want_s,
    small_sem,
    load_sem,
    want_sem,
    send_sem,
    recv_sem,
):
    hours, patch_width = sky.shape
    blocks, depth, tile = view_w.shape
    sens_blocks = sens_w.shape[0]
    per = depth // tile
    patches = patch_width // tile
    me = lax.axis_index("surf")
    far = farthest_first(n)

    def out_to(step):
        if far is None:
            return lax.rem(me + step, n)
        to = me
        for bit in (1, 2, 4):
            if step & bit:
                to = to + bit * (1 - 2 * lax.rem(me // bit, 2))
        return to

    def in_from(step):
        return lax.rem(me + n - step, n) if far is None else out_to(step)

    barrier = pltpu.get_barrier_semaphore()

    def loop(low, high, body, group):
        count = high - low
        group = next(g for g in range(min(group, count), 0, -1) if count % g == 0)

        def go(i, carry):
            for u in range(group):
                body(low + i * group + u)
            return carry

        lax.fori_loop(0, count // group, go, 0)

    def each(turn, body):
        if far is None:
            loop(1, n, lambda step: body(turn(step)), 7)
        else:
            for step in range(1, n):
                body(turn(step))

    def each_far(body):
        if far is None:
            each(out_to, body)
        else:
            for step in far:
                body(out_to(step))

    def greet(peer):
        pl.semaphore_signal(
            barrier, inc=1, device_id={"surf": peer}, device_id_type=pl.DeviceIdType.MESH
        )

    each(out_to, greet)

    surf_parts = load_parts(blocks)
    sens_parts = load_parts(sens_blocks)

    def part(hbm, vmem, parts, i, first):
        size = vmem.shape[0] // parts
        span = pl.ds(i * size, size)
        return pltpu.make_async_copy(hbm.at[span], vmem.at[span], load_sem.at[first + i])

    surf_loads = [part(surf_hbm, surf_w, surf_parts, i, 0) for i in range(surf_parts)]
    view_load = part(view_hbm, view_w, 1, 0, surf_parts)
    sens_loads = [
        part(sens_hbm, sens_w, sens_parts, i, surf_parts + 1) for i in range(sens_parts)
    ]
    small = (
        (wanted_hbm.at[0], want_own),
        (wanted_hbm.at[0], want_v.at[me]),
        (sky_hbm, sky),
        (surf_patch_hbm, surf_patch),
        (surf_count_hbm, surf_count),
        (albedo_hbm, albedo),
        (view_peer_hbm, view_peer),
        (sens_patch_hbm, sens_patch),
        (sens_count_hbm, sens_count),
        (sens_surf_hbm, sens_surf),
        (sens_weight_hbm, sens_weight),
    )
    small_loads = [
        pltpu.make_async_copy(src, dst, small_sem.at[i]) for i, (src, dst) in enumerate(small)
    ]
    early, late = small_loads[:6], small_loads[6:]
    for copy in (*early, *surf_loads, *late, *sens_loads[:2], view_load, *sens_loads[2:]):
        copy.start()

    def remote(src, dst, kind, to, mine):
        return pltpu.make_async_remote_copy(
            src_ref=src,
            dst_ref=dst.at[mine],
            send_sem=send_sem.at[kind, to],
            recv_sem=recv_sem.at[kind, mine],
            device_id={"surf": to},
            device_id_type=pl.DeviceIdType.MESH,
        )

    early[0].wait()
    pl.semaphore_wait(barrier, n - 1)
    each_far(lambda e: remote(want_own, want_v, 0, e, me).start())

    early[2].wait()
    for j in range(patches):
        sky_tab[j] = sky[:, j * tile : (j + 1) * tile]
    sky_tab[patches] = jnp.zeros((hours, tile), BF16)

    def live(patch, count, k, b):
        return jnp.where(k < count[b], patch[k, b], patches)

    def direct_block(b):
        picks = [live(surf_patch, surf_count, k, b) for k in range(per)]
        value = wide_dot(sky_tab, picks, surf_w[b])
        direct[b] = value
        rad[b] = (value * albedo[b]).astype(BF16)

    def sens_block(b):
        picks = [live(sens_patch, sens_count, k, b) for k in range(per)]
        cols = pl.ds(pl.multiple_of(b * tile, tile), tile)
        sens_out[:, cols] = wide_dot(sky_tab, picks, sens_w[b])

    for copy in (early[1], *early[3:]):
        copy.wait()
    for i, copy in enumerate(surf_loads):
        copy.wait()
        size = blocks // surf_parts
        loop(i * size, (i + 1) * size, direct_block, 4)

    for copy in late:
        copy.wait()

    each(in_from, lambda e: remote(want_own, want_v, 0, me, e).wait_recv())
    to_smem = pltpu.make_async_copy(want_v, want_s, want_sem.at[0])
    to_smem.start()
    to_smem.wait()

    def asked(e):
        return want_s[e, 0, me]

    def first_send(e):
        send_a[e] = rad[asked(e)]
        remote(send_a.at[e], slots_a, 1, e, me).start()

    each(in_from, first_send)
    slots_a[me] = rad[asked(me)]

    half = sens_parts // 2
    rows = lax.broadcasted_iota(jnp.int32, (tile, 2 * tile), 0).astype(jnp.int16)
    ones = jnp.ones((tile, 2 * tile), BF16)
    zeros = jnp.zeros((tile, 2 * tile), BF16)

    def onehot_block(r):
        cols = pl.ds(pl.multiple_of(r * tile, tile), tile)
        index = sens_surf[:, cols] - me * (blocks * tile)
        index = jnp.concatenate([index[0:1], index[1:2]], axis=1)
        index = jnp.broadcast_to(index, (tile, 2 * tile)).astype(jnp.int16)
        for s in range(blocks):
            hit = rows == index - jnp.int16(s * tile)
            onehot[r, s * tile : (s + 1) * tile, :] = jnp.where(hit, ones, zeros).astype(F8)

    def sens_part(i):
        sens_loads[i].wait()
        size = sens_blocks // sens_parts
        loop(i * size, (i + 1) * size, sens_block, 6)
        loop(i * size, (i + 1) * size, onehot_block, 1)

    for i in range(half):
        sens_part(i)

    view_load.wait()
    each(in_from, lambda e: remote(send_a.at[e], slots_a, 1, me, e).wait_recv())

    def bounced(slots, b):
        picks = [view_peer[k, b] for k in range(per)]
        return wide_dot(slots, picks, view_w[b])

    def second_value(b):
        value = direct[b] + bounced(slots_a, b)
        return (value * albedo[b]).astype(BF16)

    def second_send(e):
        send_b[e] = second_value(asked(e))
        remote(send_b.at[e], slots_b, 2, e, me).start()

    each_far(second_send)
    slots_b[me] = second_value(asked(me))

    for i in range(half, sens_parts):
        sens_part(i)

    each(in_from, lambda e: remote(send_b.at[e], slots_b, 2, me, e).wait_recv())

    group = 8 if blocks % 8 == 0 else 1

    def last_blocks(i, most):
        for u in range(group):
            b = i * group + u
            value = bounced(slots_b, b)
            cols = pl.ds(pl.multiple_of(b * tile, tile), tile)
            refl[:, cols] = value
            surf_out[:, cols] = direct[b] + value
            most = jnp.maximum(most, jnp.abs(value))
        return most

    most = lax.fori_loop(0, blocks // group, last_blocks, jnp.full((hours, tile), 1e-30, F32))
    most = jnp.max(jnp.max(most, axis=0, keepdims=True), axis=1, keepdims=True)
    gain[...] = sens_weight[...] * (most * (1 / TOP))
    rest = refl[...] * (TOP / most)
    for i in range(3):
        piece = rest.astype(F8)
        pieces[i * hours : (i + 1) * hours, :] = piece
        rest = (rest - piece.astype(F32)) * STEP

    each(out_to, lambda e: remote(want_own, want_v, 0, e, me).wait_send())
    each(out_to, lambda e: remote(send_a.at[e], slots_a, 1, e, me).wait_send())
    each(out_to, lambda e: remote(send_b.at[e], slots_b, 2, e, me).wait_send())


def load_parts(blocks):
    return 4 if blocks % 4 == 0 else 1


def local(
    sky_radiance,
    surf_coeff,
    surf_patch,
    surf_count,
    sens_coeff,
    sens_patch,
    sens_count,
    albedo,
    view_tile,
    view_peer,
    wanted,
    sens_surf,
    sens_weight,
):
    n = lax.axis_size("surf")
    hours, patch_width = sky_radiance.shape
    blocks, per, tile, _ = view_tile.shape
    sens_blocks = sens_coeff.shape[0]
    depth = per * tile
    patches = patch_width // tile

    hbm = pl.BlockSpec(memory_space=pltpu.HBM)
    vmem = pl.BlockSpec(memory_space=pltpu.VMEM)
    loads = load_parts(blocks) + 1 + load_parts(sens_blocks)
    made = pl.pallas_call(
        functools.partial(kernel, n),
        out_shape=(
            pltpu.VMEM((hours, blocks * tile), F32),
            pltpu.VMEM((hours, sens_blocks * tile), F32),
            pltpu.VMEM((3 * hours, blocks * tile), F8),
            pltpu.VMEM((sens_blocks, blocks * tile, 2 * tile), F8),
            pltpu.VMEM(sens_weight.shape, F32),
        ),
        in_specs=[hbm] * 13,
        out_specs=(vmem,) * 5,
        scratch_shapes=[
            pltpu.VMEM((hours, patch_width), BF16),
            pltpu.SMEM((per, blocks), jnp.int32),
            pltpu.SMEM((blocks,), jnp.int32),
            pltpu.SMEM((per, sens_blocks), jnp.int32),
            pltpu.SMEM((sens_blocks,), jnp.int32),
            pltpu.VMEM((blocks, 1, tile), F32),
            pltpu.SMEM((per, blocks), jnp.int32),
            pltpu.VMEM(sens_surf.shape, jnp.int32),
            pltpu.VMEM(sens_weight.shape, F32),
            pltpu.VMEM((patches + 1, hours, tile), BF16),
            pltpu.VMEM((blocks, depth, tile), BF16),
            pltpu.VMEM((sens_blocks, depth, tile), BF16),
            pltpu.VMEM((blocks, depth, tile), BF16),
            pltpu.VMEM((blocks, hours, tile), F32),
            pltpu.VMEM((blocks, hours, tile), BF16),
            pltpu.VMEM((hours, blocks * tile), F32),
            pltpu.VMEM((n, hours, tile), BF16),
            pltpu.VMEM((n, hours, tile), BF16),
            pltpu.VMEM((n, hours, tile), BF16),
            pltpu.VMEM((n, hours, tile), BF16),
            pltpu.VMEM((1, n), jnp.int32),
            pltpu.VMEM((n, 1, n), jnp.int32),
            pltpu.SMEM((n, 1, n), jnp.int32),
            pltpu.SemaphoreType.DMA((11,)),
            pltpu.SemaphoreType.DMA((loads,)),
            pltpu.SemaphoreType.DMA((2,)),
            pltpu.SemaphoreType.DMA((3, n)),
            pltpu.SemaphoreType.DMA((3, n)),
        ],
        compiler_params=pltpu.CompilerParams(
            collective_id=0, has_side_effects=True, vmem_limit_bytes=24 * 2**20
        ),
    )(
        *(
            pltpu.with_memory_space_constraint(a, pltpu.HBM)
            for a in (
                sky_radiance,
                surf_coeff.reshape(blocks, depth, tile),
                surf_patch.T,
                surf_count,
                sens_coeff.reshape(sens_blocks, depth, tile),
                sens_patch.T,
                sens_count,
                albedo.reshape(blocks, 1, tile),
                view_tile.reshape(blocks, depth, tile),
                view_peer.T,
                wanted.reshape(1, 1, n),
                sens_surf,
                sens_weight,
            )
        )
    )
    return sensors(*made)


def near(parts, surf, sens, pieces, onehot, gain, surf_hbm, sens_hbm, out, sem):
    hours = surf.shape[0]
    sens_blocks, _, tile = onehot.shape
    tile //= 2
    stores = [pltpu.make_async_copy(surf, surf_hbm, sem.at[0])]
    stores[0].start()
    size = sens_blocks // parts
    for i in range(parts):
        for r in range(i * size, (i + 1) * size):
            cols = pl.ds(r * tile, tile)
            found = jnp.dot(pieces[...], onehot[r], preferred_element_type=F32)
            found = found[:hours] + (1 / STEP) * (
                found[hours : 2 * hours] + (1 / STEP) * found[2 * hours :]
            )
            weight = gain[:, cols]
            out[:, cols] = (
                sens[:, cols]
                + weight[0:1] * found[:, :tile]
                + weight[1:2] * found[:, tile:]
            )
        cols = pl.ds(i * size * tile, size * tile)
        copy = pltpu.make_async_copy(out.at[:, cols], sens_hbm.at[:, cols], sem.at[1 + i])
        copy.start()
        stores.append(copy)
    for copy in stores:
        copy.wait()


def sensors(*arrays):
    surf, sens = arrays[:2]
    parts = load_parts(arrays[3].shape[0])
    hbm = pl.BlockSpec(memory_space=pltpu.HBM)
    vmem = pl.BlockSpec(memory_space=pltpu.VMEM)
    return pl.pallas_call(
        functools.partial(near, parts),
        out_shape=(
            jax.ShapeDtypeStruct(surf.shape, F32),
            jax.ShapeDtypeStruct(sens.shape, F32),
        ),
        in_specs=[vmem] * 5,
        out_specs=(hbm, hbm),
        scratch_shapes=[pltpu.VMEM(sens.shape, F32), pltpu.SemaphoreType.DMA((1 + parts,))],
        compiler_params=pltpu.CompilerParams(vmem_limit_bytes=8 * 2**20),
    )(*(pltpu.with_memory_space_constraint(a, pltpu.VMEM) for a in arrays))


def solution(mesh):
    in_specs = (
        P("hours", None),
        P("surf", None, None, None),
        P("surf", None),
        P("surf"),
        P("surf", None, None, None),
        P("surf", None),
        P("surf"),
        P("surf"),
        P("surf", None, None, None),
        P("surf", None),
        P("surf", None),
        P(None, "surf"),
        P(None, "surf"),
    )
    out_specs = (P("hours", "surf"), P("hours", "surf"))
    return jax.shard_map(local, mesh=mesh, in_specs=in_specs, out_specs=out_specs, check_vma=False)
```

time: 30.3 us -> 25.5 us (0.84)
  Pallas kernels: 29.5 us -> 24.7 us
    pallas_call x2, Pallas kernels: 29.5 us -> 24.7 us  [the longest x1 21.4 us: local(): pl.pallas_call(functools.partial(kernel, n), out_shape=(pltpu.VMEM((hours...]
where the time goes in v1:
time: 25.5 us; the launch traced here: 25.3 us
  Pallas kernels  24.7 us (97%)
  between operations  0.64 us (3%)
    pallas_call x1, Pallas kernels, local(): pl.pallas_call(functools.partial(kernel, n), out_shape=(pltpu.VMEM((hours...  21.4 us
    pallas_call x1, Pallas kernels, sensors(): pl.pallas_call(functools.partial(near, parts), out_shape=(jax.ShapeDtypeS...  3.3 us

profile of v1, /device:TPU:0, one launch (start us, length us, event | category | flops | bytes accessed | tf_op | source)
XLA Modules:
  0.0 25.3 jit_solution(4761100751958112659)
XLA Ops:
  0.6 21.4 %shard_map.140 = (f32[64,2048]{1,0:T(8,128)S(1)}, f32[64,3072]{1,0:T(8,128)S(1)}, f8e4m3fn[192,2048]{1,0:T(32,128)(4,1)S(1)}, f8e4m3fn[24,2048,256]{2,1,0:T(32,128)(4,1)S(1)}, f32[2,3072]{1,0:T(2,128)S(1)}) custom-call(bf16[64,2304]{1,0:T(8,128)(2,1)} %sky_hbm.1, bf16[16,1024,128]{2,1,0:T(8,128)(2,1)} %bitcast.9, s32[8,16]{1,0:T(8,128)} %bitcast.12, ...), custom_call_target="tpu_custom_call" | custom-call | tf_op jit(solution)/shard_map/pallas_call | solution.py:324
  22.0 3.3 %shard_map.141 = (f32[64,2048]{1,0:T(8,128)}, f32[64,3072]{1,0:T(8,128)}) custom-call(f32[64,2048]{1,0:T(8,128)S(1)} %get-tuple-element.7.surf, f32[64,3072]{1,0:T(8,128)S(1)} %get-tuple-element.8.sens, f8e4m3fn[192,2048]{1,0:T(32,128)(4,1)S(1)} %get-tuple-element.9.pieces, f8e4m3fn[24,2048,256]{2,1,0:T(32,128)(4,1)S(1)} %get-tuple-element.10.onehot, ...), custom_call_target="tpu_custom_call" | custom-call | tf_op jit(solution)/shard_map/pallas_call | solution.py:424

commit v2 on v1

--- a/solution.py
+++ b/solution.py
@@ -67,6 +67,7 @@
     slots_a,
     slots_b,
     want_own,
+    want_rows,
     want_v,
     want_s,
     small_sem,
@@ -144,7 +145,6 @@
     ]
     small = (
         (wanted_hbm.at[0], want_own),
-        (wanted_hbm.at[0], want_v.at[me]),
         (sky_hbm, sky),
         (surf_patch_hbm, surf_patch),
         (surf_count_hbm, surf_count),
@@ -158,7 +158,7 @@
     small_loads = [
         pltpu.make_async_copy(src, dst, small_sem.at[i]) for i, (src, dst) in enumerate(small)
     ]
-    early, late = small_loads[:6], small_loads[6:]
+    early, late = small_loads[:5], small_loads[5:]
     for copy in (*early, *surf_loads, *late, *sens_loads[:2], view_load, *sens_loads[2:]):
         copy.start()
 
@@ -173,10 +173,13 @@
         )
 
     early[0].wait()
+    for e in range(n):
+        want_rows[e] = jnp.full(want_rows.shape[1:], want_own[0, e], jnp.int32)
+    want_v[me] = want_rows[me]
     pl.semaphore_wait(barrier, n - 1)
-    each_far(lambda e: remote(want_own, want_v, 0, e, me).start())
-
-    early[2].wait()
+    each_far(lambda e: remote(want_rows.at[e], want_v, 0, e, me).start())
+
+    early[1].wait()
     for j in range(patches):
         sky_tab[j] = sky[:, j * tile : (j + 1) * tile]
     sky_tab[patches] = jnp.zeros((hours, tile), BF16)
@@ -195,7 +198,7 @@
         cols = pl.ds(pl.multiple_of(b * tile, tile), tile)
         sens_out[:, cols] = wide_dot(sky_tab, picks, sens_w[b])
 
-    for copy in (early[1], *early[3:]):
+    for copy in early[2:]:
         copy.wait()
     for i, copy in enumerate(surf_loads):
         copy.wait()
@@ -205,20 +208,15 @@
     for copy in late:
         copy.wait()
 
-    each(in_from, lambda e: remote(want_own, want_v, 0, me, e).wait_recv())
+    def first_send(e):
+        remote(want_rows.at[e], want_v, 0, me, e).wait_recv()
+        send_a[e] = rad[jnp.max(want_v[e])]
+        remote(send_a.at[e], slots_a, 1, e, me).start()
+
+    each(in_from, first_send)
+    slots_a[me] = rad[jnp.max(want_v[me])]
     to_smem = pltpu.make_async_copy(want_v, want_s, want_sem.at[0])
     to_smem.start()
-    to_smem.wait()
-
-    def asked(e):
-        return want_s[e, 0, me]
-
-    def first_send(e):
-        send_a[e] = rad[asked(e)]
-        remote(send_a.at[e], slots_a, 1, e, me).start()
-
-    each(in_from, first_send)
-    slots_a[me] = rad[asked(me)]
 
     half = sens_parts // 2
     rows = lax.broadcasted_iota(jnp.int32, (tile, 2 * tile), 0).astype(jnp.int16)
@@ -244,12 +242,16 @@
         sens_part(i)
 
     view_load.wait()
+    to_smem.wait()
     each(in_from, lambda e: remote(send_a.at[e], slots_a, 1, me, e).wait_recv())
 
     def bounced(slots, b):
         picks = [view_peer[k, b] for k in range(per)]
         return wide_dot(slots, picks, view_w[b])
 
+    def asked(e):
+        return want_s[e, 0, 0]
+
     def second_value(b):
         value = direct[b] + bounced(slots_a, b)
         return (value * albedo[b]).astype(BF16)
@@ -266,7 +268,7 @@
 
     each(in_from, lambda e: remote(send_b.at[e], slots_b, 2, me, e).wait_recv())
 
-    group = 8 if blocks % 8 == 0 else 1
+    group = next(g for g in (16, 8, 4, 2, 1) if blocks % g == 0)
 
     def last_blocks(i, most):
         for u in range(group):
@@ -287,7 +289,7 @@
         pieces[i * hours : (i + 1) * hours, :] = piece
         rest = (rest - piece.astype(F32)) * STEP
 
-    each(out_to, lambda e: remote(want_own, want_v, 0, e, me).wait_send())
+    each(out_to, lambda e: remote(want_rows.at[e], want_v, 0, e, me).wait_send())
     each(out_to, lambda e: remote(send_a.at[e], slots_a, 1, e, me).wait_send())
     each(out_to, lambda e: remote(send_b.at[e], slots_b, 2, e, me).wait_send())
 
@@ -353,10 +355,11 @@
             pltpu.VMEM((n, hours, tile), BF16),
             pltpu.VMEM((n, hours, tile), BF16),
             pltpu.VMEM((n, hours, tile), BF16),
-            pltpu.VMEM((1, n), jnp.int32),
-            pltpu.VMEM((n, 1, n), jnp.int32),
-            pltpu.SMEM((n, 1, n), jnp.int32),
-            pltpu.SemaphoreType.DMA((11,)),
+            pltpu.SMEM((1, n), jnp.int32),
+            pltpu.VMEM((n, 1, tile), jnp.int32),
+            pltpu.VMEM((n, 1, tile), jnp.int32),
+            pltpu.SMEM((n, 1, tile), jnp.int32),
+            pltpu.SemaphoreType.DMA((10,)),
             pltpu.SemaphoreType.DMA((loads,)),
             pltpu.SemaphoreType.DMA((2,)),
             pltpu.SemaphoreType.DMA((3, n)),
@@ -390,13 +393,12 @@
 
 def near(parts, surf, sens, pieces, onehot, gain, surf_hbm, sens_hbm, out, sem):
     hours = surf.shape[0]
-    sens_blocks, _, tile = onehot.shape
-    tile //= 2
+    tile = onehot.shape[2] // 2
     stores = [pltpu.make_async_copy(surf, surf_hbm, sem.at[0])]
     stores[0].start()
-    size = sens_blocks // parts
-    for i in range(parts):
-        for r in range(i * size, (i + 1) * size):
+    low = 0
+    for i, high in enumerate(parts):
+        for r in range(low, high):
             cols = pl.ds(r * tile, tile)
             found = jnp.dot(pieces[...], onehot[r], preferred_element_type=F32)
             found = found[:hours] + (1 / STEP) * (
@@ -408,17 +410,19 @@
                 + weight[0:1] * found[:, :tile]
                 + weight[1:2] * found[:, tile:]
             )
-        cols = pl.ds(i * size * tile, size * tile)
+        cols = pl.ds(low * tile, (high - low) * tile)
         copy = pltpu.make_async_copy(out.at[:, cols], sens_hbm.at[:, cols], sem.at[1 + i])
         copy.start()
         stores.append(copy)
+        low = high
     for copy in stores:
         copy.wait()
 
 
 def sensors(*arrays):
     surf, sens = arrays[:2]
-    parts = load_parts(arrays[3].shape[0])
+    count = arrays[3].shape[0]
+    parts = [*range(6, count - 5, 6), count - 2, count] if count > 6 else [count]
     hbm = pl.BlockSpec(memory_space=pltpu.HBM)
     vmem = pl.BlockSpec(memory_space=pltpu.VMEM)
     return pl.pallas_call(
@@ -429,7 +433,7 @@
         ),
         in_specs=[vmem] * 5,
         out_specs=(hbm, hbm),
-        scratch_shapes=[pltpu.VMEM(sens.shape, F32), pltpu.SemaphoreType.DMA((1 + parts,))],
+        scratch_shapes=[pltpu.VMEM(sens.shape, F32), pltpu.SemaphoreType.DMA((1 + len(parts),))],
         compiler_params=pltpu.CompilerParams(vmem_limit_bytes=8 * 2**20),
     )(*(pltpu.with_memory_space_constraint(a, pltpu.VMEM) for a in arrays))
 

time: 25.5 us -> 24.7 us (0.969)
  Pallas kernels: 24.7 us -> 23.9 us
    pallas_call x1, Pallas kernels: 21.4 us -> 20.7 us  [local(): pl.pallas_call(functools.partial(kernel, n), out_shape=(pltpu.VMEM((hours...]
where the time goes in v2:
time: 24.7 us; the launch traced here: 24.6 us
  Pallas kernels  23.9 us (97%)
  between operations  0.64 us (3%)
    pallas_call x1, Pallas kernels, local(): pl.pallas_call(functools.partial(kernel, n), out_shape=(pltpu.VMEM((hours...  20.7 us
    pallas_call x1, Pallas kernels, sensors(): pl.pallas_call(functools.partial(near, parts), out_shape=(jax.ShapeDtypeS...  3.26 us

profile of v2, /device:TPU:0, one launch (start us, length us, event | category | flops | bytes accessed | tf_op | source)
XLA Modules:
  0.0 24.6 jit_solution(592240446929762754)
XLA Ops:
  0.6 20.7 %shard_map.140 = (f32[64,2048]{1,0:T(8,128)S(1)}, f32[64,3072]{1,0:T(8,128)S(1)}, f8e4m3fn[192,2048]{1,0:T(32,128)(4,1)S(1)}, f8e4m3fn[24,2048,256]{2,1,0:T(32,128)(4,1)S(1)}, f32[2,3072]{1,0:T(2,128)S(1)}) custom-call(bf16[64,2304]{1,0:T(8,128)(2,1)} %sky_hbm.1, bf16[16,1024,128]{2,1,0:T(8,128)(2,1)} %bitcast.9, s32[8,16]{1,0:T(8,128)} %bitcast.12, ...), custom_call_target="tpu_custom_call" | custom-call | tf_op jit(solution)/shard_map/pallas_call | solution.py:326
  21.3 3.3 %shard_map.141 = (f32[64,2048]{1,0:T(8,128)}, f32[64,3072]{1,0:T(8,128)}) custom-call(f32[64,2048]{1,0:T(8,128)S(1)} %get-tuple-element.7.surf, f32[64,3072]{1,0:T(8,128)S(1)} %get-tuple-element.8.sens, f8e4m3fn[192,2048]{1,0:T(32,128)(4,1)S(1)} %get-tuple-element.9.pieces, f8e4m3fn[24,2048,256]{2,1,0:T(32,128)(4,1)S(1)} %get-tuple-element.10.onehot, ...), custom_call_target="tpu_custom_call" | custom-call | tf_op jit(solution)/shard_map/pallas_call | solution.py:428

commit v3 on v2

--- a/solution.py
+++ b/solution.py
@@ -43,9 +43,11 @@
     sens_weight_hbm,
     surf_out,
     sens_out,
-    pieces,
+    refl,
+    most,
     onehot,
-    gain,
+    place,
+    weight,
     sky,
     surf_patch,
     surf_count,
@@ -54,14 +56,12 @@
     albedo,
     view_peer,
     sens_surf,
-    sens_weight,
     sky_tab,
     surf_w,
     sens_w,
     view_w,
     direct,
     rad,
-    refl,
     send_a,
     send_b,
     slots_a,
@@ -128,7 +128,7 @@
             barrier, inc=1, device_id={"surf": peer}, device_id_type=pl.DeviceIdType.MESH
         )
 
-    each(out_to, greet)
+    each_far(greet)
 
     surf_parts = load_parts(blocks)
     sens_parts = load_parts(sens_blocks)
@@ -153,13 +153,13 @@
         (sens_patch_hbm, sens_patch),
         (sens_count_hbm, sens_count),
         (sens_surf_hbm, sens_surf),
-        (sens_weight_hbm, sens_weight),
+        (sens_weight_hbm, weight),
     )
     small_loads = [
         pltpu.make_async_copy(src, dst, small_sem.at[i]) for i, (src, dst) in enumerate(small)
     ]
     early, late = small_loads[:5], small_loads[5:]
-    for copy in (*early, *surf_loads, *late, *sens_loads[:2], view_load, *sens_loads[2:]):
+    for copy in (*early, *surf_loads, *late):
         copy.start()
 
     def remote(src, dst, kind, to, mine):
@@ -207,6 +207,9 @@
 
     for copy in late:
         copy.wait()
+    for copy in (*sens_loads[:2], view_load, *sens_loads[2:]):
+        copy.start()
+    place[...] = sens_surf[...] - me * (blocks * tile)
 
     def first_send(e):
         remote(want_rows.at[e], want_v, 0, me, e).wait_recv()
@@ -225,7 +228,7 @@
 
     def onehot_block(r):
         cols = pl.ds(pl.multiple_of(r * tile, tile), tile)
-        index = sens_surf[:, cols] - me * (blocks * tile)
+        index = place[:, cols]
         index = jnp.concatenate([index[0:1], index[1:2]], axis=1)
         index = jnp.broadcast_to(index, (tile, 2 * tile)).astype(jnp.int16)
         for s in range(blocks):
@@ -270,24 +273,17 @@
 
     group = next(g for g in (16, 8, 4, 2, 1) if blocks % g == 0)
 
-    def last_blocks(i, most):
+    def last_blocks(i, top):
         for u in range(group):
             b = i * group + u
             value = bounced(slots_b, b)
             cols = pl.ds(pl.multiple_of(b * tile, tile), tile)
             refl[:, cols] = value
             surf_out[:, cols] = direct[b] + value
-            most = jnp.maximum(most, jnp.abs(value))
-        return most
-
-    most = lax.fori_loop(0, blocks // group, last_blocks, jnp.full((hours, tile), 1e-30, F32))
-    most = jnp.max(jnp.max(most, axis=0, keepdims=True), axis=1, keepdims=True)
-    gain[...] = sens_weight[...] * (most * (1 / TOP))
-    rest = refl[...] * (TOP / most)
-    for i in range(3):
-        piece = rest.astype(F8)
-        pieces[i * hours : (i + 1) * hours, :] = piece
-        rest = (rest - piece.astype(F32)) * STEP
+            top = jnp.maximum(top, jnp.abs(value))
+        return top
+
+    most[...] = lax.fori_loop(0, blocks // group, last_blocks, jnp.full((hours, tile), 1e-30, F32))
 
     each(out_to, lambda e: remote(want_rows.at[e], want_v, 0, e, me).wait_send())
     each(out_to, lambda e: remote(send_a.at[e], slots_a, 1, e, me).wait_send())
@@ -328,12 +324,14 @@
         out_shape=(
             pltpu.VMEM((hours, blocks * tile), F32),
             pltpu.VMEM((hours, sens_blocks * tile), F32),
-            pltpu.VMEM((3 * hours, blocks * tile), F8),
+            pltpu.VMEM((hours, blocks * tile), F32),
+            pltpu.VMEM((hours, tile), F32),
             pltpu.VMEM((sens_blocks, blocks * tile, 2 * tile), F8),
+            pltpu.VMEM(sens_surf.shape, jnp.int32),
             pltpu.VMEM(sens_weight.shape, F32),
         ),
         in_specs=[hbm] * 13,
-        out_specs=(vmem,) * 5,
+        out_specs=(vmem,) * 7,
         scratch_shapes=[
             pltpu.VMEM((hours, patch_width), BF16),
             pltpu.SMEM((per, blocks), jnp.int32),
@@ -343,14 +341,12 @@
             pltpu.VMEM((blocks, 1, tile), F32),
             pltpu.SMEM((per, blocks), jnp.int32),
             pltpu.VMEM(sens_surf.shape, jnp.int32),
-            pltpu.VMEM(sens_weight.shape, F32),
             pltpu.VMEM((patches + 1, hours, tile), BF16),
             pltpu.VMEM((blocks, depth, tile), BF16),
             pltpu.VMEM((sens_blocks, depth, tile), BF16),
             pltpu.VMEM((blocks, depth, tile), BF16),
             pltpu.VMEM((blocks, hours, tile), F32),
             pltpu.VMEM((blocks, hours, tile), BF16),
-            pltpu.VMEM((hours, blocks * tile), F32),
             pltpu.VMEM((n, hours, tile), BF16),
             pltpu.VMEM((n, hours, tile), BF16),
             pltpu.VMEM((n, hours, tile), BF16),
@@ -391,25 +387,70 @@
     return sensors(*made)
 
 
-def near(parts, surf, sens, pieces, onehot, gain, surf_hbm, sens_hbm, out, sem):
-    hours = surf.shape[0]
+def near(
+    parts,
+    surf,
+    sens,
+    refl,
+    most,
+    onehot,
+    place,
+    weight,
+    surf_hbm,
+    sens_hbm,
+    out,
+    pieces,
+    sem,
+):
+    hours, width = refl.shape
     tile = onehot.shape[2] // 2
     stores = [pltpu.make_async_copy(surf, surf_hbm, sem.at[0])]
     stores[0].start()
+
+    top = jnp.max(jnp.max(most[...], axis=0, keepdims=True), axis=1, keepdims=True)
+    rest = refl[...] * (TOP / top)
+    for i in range(3):
+        piece = rest.astype(F8)
+        pieces[i * hours : (i + 1) * hours, :] = piece
+        rest = (rest - piece.astype(F32)) * STEP
+    back = top * (1 / TOP)
+
+    def by_matmul(cols, r):
+        found = jnp.dot(pieces[...], onehot[r], preferred_element_type=F32)
+        found = found[:hours] + (1 / STEP) * (
+            found[hours : 2 * hours] + (1 / STEP) * found[2 * hours :]
+        )
+        gain = weight[:, cols] * back
+        out[:, cols] = (
+            sens[:, cols] + gain[0:1] * found[:, :tile] + gain[1:2] * found[:, tile:]
+        )
+
+    def by_gather(cols):
+        block = place[:, cols] // tile
+        lane = place[:, cols] - block * tile
+        rows = 8
+        shape = (rows, tile)
+        for h in range(0, hours, rows):
+            total = sens[h : h + rows, cols]
+            for j in range(2):
+                lanes = jnp.broadcast_to(lane[j : j + 1], shape)
+                picked = jnp.broadcast_to(block[j : j + 1], shape)
+                found = jnp.zeros(shape, F32)
+                for s in range(width // tile):
+                    part = refl[h : h + rows, s * tile : (s + 1) * tile]
+                    part = jnp.take_along_axis(part, lanes, axis=1)
+                    found = jnp.where(picked == s, part, found)
+                total = total + jnp.broadcast_to(weight[j : j + 1, cols], shape) * found
+            out[h : h + rows, cols] = total
+
     low = 0
     for i, high in enumerate(parts):
         for r in range(low, high):
             cols = pl.ds(r * tile, tile)
-            found = jnp.dot(pieces[...], onehot[r], preferred_element_type=F32)
-            found = found[:hours] + (1 / STEP) * (
-                found[hours : 2 * hours] + (1 / STEP) * found[2 * hours :]
-            )
-            weight = gain[:, cols]
-            out[:, cols] = (
-                sens[:, cols]
-                + weight[0:1] * found[:, :tile]
-                + weight[1:2] * found[:, tile:]
-            )
+            if r == 0 or (r % 4 == 3 and r < parts[-1] - 4):
+                by_gather(cols)
+            else:
+                by_matmul(cols, r)
         cols = pl.ds(low * tile, (high - low) * tile)
         copy = pltpu.make_async_copy(out.at[:, cols], sens_hbm.at[:, cols], sem.at[1 + i])
         copy.start()
@@ -420,8 +461,9 @@
 
 
 def sensors(*arrays):
-    surf, sens = arrays[:2]
-    count = arrays[3].shape[0]
+    surf, sens, refl = arrays[:3]
+    hours, width = refl.shape
+    count = arrays[4].shape[0]
     parts = [*range(6, count - 5, 6), count - 2, count] if count > 6 else [count]
     hbm = pl.BlockSpec(memory_space=pltpu.HBM)
     vmem = pl.BlockSpec(memory_space=pltpu.VMEM)
@@ -431,9 +473,13 @@
             jax.ShapeDtypeStruct(surf.shape, F32),
             jax.ShapeDtypeStruct(sens.shape, F32),
         ),
-        in_specs=[vmem] * 5,
+        in_specs=[vmem] * 7,
         out_specs=(hbm, hbm),
-        scratch_shapes=[pltpu.VMEM(sens.shape, F32), pltpu.SemaphoreType.DMA((1 + len(parts),))],
+        scratch_shapes=[
+            pltpu.VMEM(sens.shape, F32),
+            pltpu.VMEM((3 * hours, width), F8),
+            pltpu.SemaphoreType.DMA((1 + len(parts),)),
+        ],
         compiler_params=pltpu.CompilerParams(vmem_limit_bytes=8 * 2**20),
     )(*(pltpu.with_memory_space_constraint(a, pltpu.VMEM) for a in arrays))
 

time: 24.7 us -> 23.8 us (0.964)
  Pallas kernels: 23.9 us -> 23 us
    pallas_call x1, Pallas kernels: 20.7 us -> 20.2 us  [local(): pl.pallas_call(functools.partial(kernel, n), out_shape=(pltpu.VMEM((hours...]
    pallas_call x1, Pallas kernels: 3.26 us -> 2.84 us  [sensors(): pl.pallas_call(functools.partial(near, parts), out_shape=(jax.ShapeDtypeS...]
where the time goes in v3:
time: 23.8 us; the launch traced here: 23.7 us
  Pallas kernels  23 us (97%)
  between operations  0.64 us (3%)
    pallas_call x1, Pallas kernels, local(): pl.pallas_call(functools.partial(kernel, n), out_shape=(pltpu.VMEM((hours...  20.2 us
    pallas_call x1, Pallas kernels, sensors(): pl.pallas_call(functools.partial(near, parts), out_shape=(jax.ShapeDtypeS...  2.84 us

profile of v3, /device:TPU:0, one launch (start us, length us, event | category | flops | bytes accessed | tf_op | source)
XLA Modules:
  0.0 23.7 jit_solution(16752872694136226888)
XLA Ops:
  0.6 20.2 %shard_map.140 = (f32[64,2048]{1,0:T(8,128)S(1)}, f32[64,3072]{1,0:T(8,128)S(1)}, f32[64,2048]{1,0:T(8,128)S(1)}, f32[64,128]{1,0:T(8,128)S(1)}, f8e4m3fn[24,204...) custom-call(bf16[64,2304]{1,0:T(8,128)(2,1)} %sky_hbm.1, bf16[16,1024,128]{2,1,0:T(8,128)(2,1)} %bitcast.9, ...), custom_call_target="tpu_custom_call" | custom-call | tf_op jit(solution)/shard_map/pallas_call | solution.py:322
  20.8 2.8 %shard_map.141 = (f32[64,2048]{1,0:T(8,128)}, f32[64,3072]{1,0:T(8,128)}) custom-call(f32[64,2048]{1,0:T(8,128)S(1)} %get-tuple-element.9.surf, f32[64,3072]{1,0:T(8,128)S(1)} %get-tuple-element.10.sens, f32[64,2048]{1,0:T(8,128)S(1)} %get-tuple-element.11.refl, f32[64,128]{1,0:T(8,128)S(1)} %get-tuple-element.12.most, ...), custom_call_target="tpu_custom_call" | custom-call | tf_op jit(solution)/shard_map/pallas_call | solution.py:470

commit v4 on v3

--- a/solution.py
+++ b/solution.py
@@ -263,12 +263,24 @@
         send_b[e] = second_value(asked(e))
         remote(send_b.at[e], slots_b, 2, e, me).start()
 
-    each_far(second_send)
+    if far is None:
+        each_far(second_send)
+    else:
+        peers = [out_to(step) for step in far]
+        cuts = sorted({0, *(c for c in (2, 4) if c < n - 1), n - 1})
+        for low, high in zip(cuts, cuts[1:]):
+            values = [second_value(asked(e)) for e in peers[low:high]]
+            for e, value in zip(peers[low:high], values):
+                send_b[e] = value
+            for e in peers[low:high]:
+                remote(send_b.at[e], slots_b, 2, e, me).start()
     slots_b[me] = second_value(asked(me))
 
     for i in range(half, sens_parts):
         sens_part(i)
 
+    each(out_to, lambda e: remote(want_rows.at[e], want_v, 0, e, me).wait_send())
+    each(out_to, lambda e: remote(send_a.at[e], slots_a, 1, e, me).wait_send())
     each(in_from, lambda e: remote(send_b.at[e], slots_b, 2, me, e).wait_recv())
 
     group = next(g for g in (16, 8, 4, 2, 1) if blocks % g == 0)
@@ -285,8 +297,6 @@
 
     most[...] = lax.fori_loop(0, blocks // group, last_blocks, jnp.full((hours, tile), 1e-30, F32))
 
-    each(out_to, lambda e: remote(want_rows.at[e], want_v, 0, e, me).wait_send())
-    each(out_to, lambda e: remote(send_a.at[e], slots_a, 1, e, me).wait_send())
     each(out_to, lambda e: remote(send_b.at[e], slots_b, 2, e, me).wait_send())
 
 

time: 23.8 us -> 23.8 us (level)
  no operation moved by 1% of the time
where the time goes in v4:
time: 23.8 us; the launch traced here: 23.6 us
  Pallas kernels  23 us (97%)
  between operations  0.64 us (3%)
    pallas_call x1, Pallas kernels, local(): pl.pallas_call(functools.partial(kernel, n), out_shape=(pltpu.VMEM((hours...  20.1 us
    pallas_call x1, Pallas kernels, sensors(): pl.pallas_call(functools.partial(near, parts), out_shape=(jax.ShapeDtypeS...  2.84 us

profile of v4, /device:TPU:0, one launch (start us, length us, event | category | flops | bytes accessed | tf_op | source)
XLA Modules:
  0.0 23.6 jit_solution(5208539560049046857)
XLA Ops:
  0.6 20.1 %shard_map.140 = (f32[64,2048]{1,0:T(8,128)S(1)}, f32[64,3072]{1,0:T(8,128)S(1)}, f32[64,2048]{1,0:T(8,128)S(1)}, f32[64,128]{1,0:T(8,128)S(1)}, f8e4m3fn[24,204...) custom-call(bf16[64,2304]{1,0:T(8,128)(2,1)} %sky_hbm.1, bf16[16,1024,128]{2,1,0:T(8,128)(2,1)} %bitcast.9, ...), custom_call_target="tpu_custom_call" | custom-call | tf_op jit(solution)/shard_map/pallas_call | solution.py:332
  20.8 2.8 %shard_map.141 = (f32[64,2048]{1,0:T(8,128)}, f32[64,3072]{1,0:T(8,128)}) custom-call(f32[64,2048]{1,0:T(8,128)S(1)} %get-tuple-element.9.surf, f32[64,3072]{1,0:T(8,128)S(1)} %get-tuple-element.10.sens, f32[64,2048]{1,0:T(8,128)S(1)} %get-tuple-element.11.refl, f32[64,128]{1,0:T(8,128)S(1)} %get-tuple-element.12.most, ...), custom_call_target="tpu_custom_call" | custom-call | tf_op jit(solution)/shard_map/pallas_call | solution.py:480

commit v5 on v4

--- a/solution.py
+++ b/solution.py
@@ -23,7 +23,7 @@
 def farthest_first(n):
     if n > 8 or n & (n - 1):
         return None
-    return [*range(n - 1, 0, -2), *range(n - 2, 0, -2)]
+    return [*range(n - 1, 0, -1)]
 
 
 def kernel(

time: 23.8 us -> 23.4 us (0.983)
  Pallas kernels: 23 us -> 22.6 us
    pallas_call x1, Pallas kernels: 20.1 us -> 19.8 us  [local(): pl.pallas_call(functools.partial(kernel, n), out_shape=(pltpu.VMEM((hours...]
where the time goes in v5:
time: 23.4 us; the launch traced here: 23.2 us
  Pallas kernels  22.6 us (97%)
  between operations  0.64 us (3%)
    pallas_call x1, Pallas kernels, local(): pl.pallas_call(functools.partial(kernel, n), out_shape=(pltpu.VMEM((hours...  19.8 us
    pallas_call x1, Pallas kernels, sensors(): pl.pallas_call(functools.partial(near, parts), out_shape=(jax.ShapeDtypeS...  2.84 us

profile of v5, /device:TPU:0, one launch (start us, length us, event | category | flops | bytes accessed | tf_op | source)
XLA Modules:
  0.0 23.2 jit_solution(5745538930015327035)
XLA Ops:
  0.6 19.8 %shard_map.140 = (f32[64,2048]{1,0:T(8,128)S(1)}, f32[64,3072]{1,0:T(8,128)S(1)}, f32[64,2048]{1,0:T(8,128)S(1)}, f32[64,128]{1,0:T(8,128)S(1)}, f8e4m3fn[24,204...) custom-call(bf16[64,2304]{1,0:T(8,128)(2,1)} %sky_hbm.1, bf16[16,1024,128]{2,1,0:T(8,128)(2,1)} %bitcast.9, ...), custom_call_target="tpu_custom_call" | custom-call | tf_op jit(solution)/shard_map/pallas_call | solution.py:332
  20.4 2.8 %shard_map.141 = (f32[64,2048]{1,0:T(8,128)}, f32[64,3072]{1,0:T(8,128)}) custom-call(f32[64,2048]{1,0:T(8,128)S(1)} %get-tuple-element.9.surf, f32[64,3072]{1,0:T(8,128)S(1)} %get-tuple-element.10.sens, f32[64,2048]{1,0:T(8,128)S(1)} %get-tuple-element.11.refl, f32[64,128]{1,0:T(8,128)S(1)} %get-tuple-element.12.most, ...), custom_call_target="tpu_custom_call" | custom-call | tf_op jit(solution)/shard_map/pallas_call | solution.py:480

commit v6 on v5

--- a/solution.py
+++ b/solution.py
@@ -216,7 +216,19 @@
         send_a[e] = rad[jnp.max(want_v[e])]
         remote(send_a.at[e], slots_a, 1, e, me).start()
 
-    each(in_from, first_send)
+    if far is None:
+        each(in_from, first_send)
+    else:
+        cuts = sorted({1, *(c for c in (3, 5) if c < n), n})
+        for low, high in zip(cuts, cuts[1:]):
+            peers = [in_from(step) for step in range(low, high)]
+            for e in peers:
+                remote(want_rows.at[e], want_v, 0, me, e).wait_recv()
+            picks = [jnp.max(want_v[e]) for e in peers]
+            for e, pick in zip(peers, picks):
+                send_a[e] = rad[pick]
+            for e in peers:
+                remote(send_a.at[e], slots_a, 1, e, me).start()
     slots_a[me] = rad[jnp.max(want_v[me])]
     to_smem = pltpu.make_async_copy(want_v, want_s, want_sem.at[0])
     to_smem.start()

time: 23.4 us -> 23.3 us (level)
  no operation moved by 1% of the time
where the time goes in v6:
time: 23.3 us; the launch traced here: 23.1 us
  Pallas kernels  22.5 us (97%)
  between operations  0.64 us (3%)
    pallas_call x1, Pallas kernels, local(): pl.pallas_call(functools.partial(kernel, n), out_shape=(pltpu.VMEM((hours...  19.7 us
    pallas_call x1, Pallas kernels, sensors(): pl.pallas_call(functools.partial(near, parts), out_shape=(jax.ShapeDtypeS...  2.84 us

profile of v6, /device:TPU:0, one launch (start us, length us, event | category | flops | bytes accessed | tf_op | source)
XLA Modules:
  0.0 23.1 jit_solution(1915729721592880820)
XLA Ops:
  0.6 19.7 %shard_map.140 = (f32[64,2048]{1,0:T(8,128)S(1)}, f32[64,3072]{1,0:T(8,128)S(1)}, f32[64,2048]{1,0:T(8,128)S(1)}, f32[64,128]{1,0:T(8,128)S(1)}, f8e4m3fn[24,204...) custom-call(bf16[64,2304]{1,0:T(8,128)(2,1)} %sky_hbm.1, bf16[16,1024,128]{2,1,0:T(8,128)(2,1)} %bitcast.9, ...), custom_call_target="tpu_custom_call" | custom-call | tf_op jit(solution)/shard_map/pallas_call | solution.py:344
  20.3 2.8 %shard_map.141 = (f32[64,2048]{1,0:T(8,128)}, f32[64,3072]{1,0:T(8,128)}) custom-call(f32[64,2048]{1,0:T(8,128)S(1)} %get-tuple-element.9.surf, f32[64,3072]{1,0:T(8,128)S(1)} %get-tuple-element.10.sens, f32[64,2048]{1,0:T(8,128)S(1)} %get-tuple-element.11.refl, f32[64,128]{1,0:T(8,128)S(1)} %get-tuple-element.12.most, ...), custom_call_target="tpu_custom_call" | custom-call | tf_op jit(solution)/shard_map/pallas_call | solution.py:492
